TPU v7x, 32 devices: a whole 2x2x4 slice. The times are simulated.
32 devices in a mesh: groups: 2 (over x), node: 16 (over z, y, core).
Axes of the slice: x: 2, y: 2, z: 4, core: 2. Of those that a mesh axis runs over, the one named last changes fastest.
Arguments:
- mixer_input: bfloat16 [256, 4096], P(('groups', 'node')), parts along dimension 0, may hold values from -6 to 6
- chosen_experts: int32 [256, 8], P(('groups', 'node')), parts along dimension 0, may hold values from 0 to 7, as said below
- route_weight: float32 [256, 8], P(('groups', 'node')), parts along dimension 0, may hold values from 0.1 to 1
- gate_weight: bfloat16 [16, 4096, 384], P('node'), may hold values from -0.09375 to 0.09375
- up_weight: bfloat16 [16, 4096, 384], P('node'), may hold values from -0.09375 to 0.09375
- down_weight: bfloat16 [16, 384, 4096], P('node'), may hold values from -0.21875 to 0.21875
- queries: bfloat16 [128, 64, 128], P(('groups', 'node')), parts along dimension 0, may hold values from -6 to 6
- fresh_key: bfloat16 [128, 4, 128], P(('groups', 'node')), parts along dimension 0, may hold values from -15 to 15
- fresh_value: bfloat16 [128, 4, 128], P(('groups', 'node')), parts along dimension 0, may hold values from -6 to 6
- cache_key: bfloat16 [128, 4, 256, 128], P(('groups', 'node')), parts along dimension 0, may hold values from -64 to 64
- cache_value: bfloat16 [128, 4, 256, 128], P(('groups', 'node')), parts along dimension 0, may hold values from -6 to 6
- lengths: int32 [128], P(('groups', 'node')), parts along dimension 0, may hold values from 2 to 256, as said below
Outputs:
- expert_mix: bfloat16 [256, 4096], P(('groups', 'node')), parts along dimension 0
- attended: bfloat16 [128, 64, 128], P(('groups', 'node')), parts along dimension 0
There are 2 independent parts, one for each index of `groups`. A program takes and returns all parts, laid end to end along the dimension named above; an argument that names none is the same for every part. Nothing has to cross between parts.
Inputs may be any that keep to these rules, and one draw needn't show every extreme that they name: `chosen_experts`: each row names 8 different experts; among the rows of one device no expert is named more than 8 times, and some expert is named exactly 8 times by the rows of every device. `lengths`: some sequence holds all 256 positions.
All inputs are finite; a program needn't handle non-finite values.
Results may differ from a plain program's by a relative error of at most 0.0058.
Values may be sent and summed in bfloat16 or wider, within the bound.
A program may use at most 64 MiB of HBM per device.

v0:
```python
import jax
import jax.numpy as jnp
from jax import lax
from jax.sharding import PartitionSpec as P


def from_partner(block, axis, bit):
    count = lax.axis_size(axis)
    route = []
    for low in range(count):
        high = low | 1 << bit
        if high != low and high < count:
            route += [(low, high), (high, low)]
    return lax.ppermute(block, axis, route)


def attention_block(queries, fresh_key, fresh_value, cache_key, cache_value, lengths):
    seq_count, head_count, head_width = queries.shape
    key_heads = cache_key.shape[1]
    context = cache_key.shape[2]
    grouped = queries.reshape(seq_count, key_heads, head_count // key_heads, head_width)
    scaling = head_width ** (-0.5)
    scores = (
        jnp.einsum("skgd,skcd->skgc", grouped, cache_key, preferred_element_type=jnp.float32)
        * scaling
    )
    own_score = (
        jnp.einsum("skgd,skd->skg", grouped, fresh_key, preferred_element_type=jnp.float32)
        * scaling
    )
    usable = jnp.arange(context, dtype=jnp.int32)[None, :] < lengths[:, None]
    masked = jnp.where(usable[:, None, None, :], scores, -jnp.inf)
    top_score = jnp.maximum(jnp.max(masked, axis=3), own_score)
    prob_rows = jnp.exp(masked - top_score[..., None])
    own_prob = jnp.exp(own_score - top_score)
    denominator = jnp.sum(prob_rows, axis=3) + own_prob
    own_low = lax.optimization_barrier(own_prob.astype(jnp.bfloat16)).astype(jnp.float32)
    numerator = jnp.einsum(
        "skgc,skcd->skgd",
        prob_rows.astype(jnp.bfloat16),
        cache_value,
        preferred_element_type=jnp.float32,
    )
    numerator = numerator + own_low[..., None] * fresh_value.astype(jnp.float32)[:, :, None, :]
    return (
        (numerator / denominator[..., None])
        .astype(jnp.bfloat16)
        .reshape(seq_count, head_count, head_width)
    )


def slot_ranks(chosen_experts, expert_count):
    token_count, top_count = chosen_experts.shape
    flat_ids = chosen_experts.reshape(token_count * top_count, 1)
    onehot = (flat_ids == jnp.arange(expert_count, dtype=jnp.int32)[None, :]).astype(jnp.int32)
    before = jnp.cumsum(onehot, axis=0) - onehot
    return jnp.sum(before * onehot, axis=1).reshape(token_count, top_count)


def expert_layer(row_block, gate_weight, up_weight, down_weight):
    gate_out = jnp.dot(row_block, gate_weight[0], preferred_element_type=jnp.float32)
    up_out = jnp.dot(row_block, up_weight[0], preferred_element_type=jnp.float32)
    hidden = (jax.nn.silu(gate_out) * up_out).astype(jnp.bfloat16)
    return jnp.dot(hidden, down_weight[0], preferred_element_type=jnp.float32)


def body(
    mixer_input,
    chosen_experts,
    route_weight,
    gate_weight,
    up_weight,
    down_weight,
    queries,
    fresh_key,
    fresh_value,
    cache_key,
    cache_value,
    lengths,
):
    node_count = lax.axis_size("node")
    expert_count = node_count // 2
    token_count, top_count = chosen_experts.shape
    model_width = mixer_input.shape[1]
    capacity = min(token_count, max(2, 2 * token_count * top_count // expert_count))
    half_cap = capacity // 2
    position = lax.axis_index("node")
    parity = position % 2
    slot_rank = slot_ranks(chosen_experts, expert_count)
    slot_codes = chosen_experts * capacity + slot_rank
    attended = attention_block(queries, fresh_key, fresh_value, cache_key, cache_value, lengths)
    slots_all = jnp.arange(expert_count * capacity, dtype=jnp.int32)
    pick_table = jnp.any(slot_codes[None, :, :] == slots_all[:, None, None], axis=2).astype(
        jnp.bfloat16
    )
    packed = jnp.dot(pick_table, mixer_input, preferred_element_type=jnp.float32).astype(
        jnp.bfloat16
    )
    doubled = jnp.broadcast_to(
        packed.reshape(expert_count, 1, capacity, model_width),
        (expert_count, 2, capacity, model_width),
    )
    arrived = lax.all_to_all(
        doubled.reshape(node_count, capacity, model_width),
        "node",
        split_axis=0,
        concat_axis=0,
        tiled=True,
    )
    partial_value = expert_layer(
        arrived.reshape(node_count * capacity, model_width), gate_weight, up_weight, down_weight
    )
    partial_value = partial_value.reshape(node_count, 2, half_cap, model_width)
    kept_half = jnp.where(parity == 0, partial_value[:, 0], partial_value[:, 1])
    outgoing = jnp.where(parity == 0, partial_value[:, 1], partial_value[:, 0])
    incoming = from_partner(outgoing, "node", 0)
    summed = (kept_half + incoming).astype(jnp.bfloat16)
    returned = lax.all_to_all(summed, "node", split_axis=0, concat_axis=0, tiled=True)
    results = returned.reshape(expert_count * capacity, model_width)
    picked = (
        jnp.take(results, slot_codes.reshape(-1), axis=0)
        .reshape(token_count, top_count, model_width)
        .astype(jnp.float32)
    )
    share_norm = route_weight / jnp.sum(route_weight, axis=1, keepdims=True)
    mixture = jnp.sum(share_norm[:, :, None] * picked, axis=1).astype(jnp.bfloat16)
    return (mixture, attended)


def solution(mesh):
    in_specs = (
        P(("groups", "node"), None),
        P(("groups", "node"), None),
        P(("groups", "node"), None),
        P("node", None, None),
        P("node", None, None),
        P("node", None, None),
        P(("groups", "node"), None, None),
        P(("groups", "node"), None, None),
        P(("groups", "node"), None, None),
        P(("groups", "node"), None, None, None),
        P(("groups", "node"), None, None, None),
        P(("groups", "node")),
    )
    out_specs = (P(("groups", "node"), None), P(("groups", "node"), None, None))
    return jax.shard_map(body, mesh=mesh, in_specs=in_specs, out_specs=out_specs, check_vma=False)
```

profile of v0, /device:TPU:0, one launch (start us, length us, event | category | flops | bytes accessed | tf_op | source)
XLA Modules:
  0.0 74.5 jit_solution(13462651477829642627)
XLA Ops:
  0.6 0.0 copy-start
  0.6 0.9 %eq.34 = s32[64]{0:T(128)S(1)} reshape(s32[8,8]{1,0:T(8,128)} %param.13) | data formatting | bytes 512 | tf_op jit(solution)/shard_map/eq | solution.py:55
  1.6 0.1 fusion.24
  1.6 0.1 reduce_window_sum.11
  1.7 0.2 select_reduce_fusion
  1.9 0.1 reshape.99
  2.0 0.7 compare_and_fusion
  2.7 0.1 fusion.25
  2.8 1.2 %fusion = bf16[8,8,4096]{2,1,0:T(8,128)(2,1)S(1)} fusion(pred[64,8]{0,1:T(8,128)(4,1)S(1)} %fusion.25, bf16[8,4096]{1,0:T(8,128)(2,1)} %param.12), kind=kOutput, calls=%fused_computation.2 | convolution fusion | flops 4456448 | bytes 590336 | tf_op jit(solution)/shard_map/dot_general | solution.py:96
  4.0 1.1 %broadcast_in_dim.28 = bf16[8,2,8,4096]{3,2,1,0:T(8,128)(2,1)} broadcast(bf16[8,8,4096]{2,1,0:T(8,128)(2,1)S(1)} %fusion), dimensions={0,2,3} | broadcast | bytes 1572864 | tf_op jit(solution)/shard_map/broadcast_in_dim | solution.py:99
  5.1 7.4 %all-to-all-start = ((bf16[16,8,4096]{2,1,0:T(8,128)(2,1)}), bf16[16,8,4096]{2,1,0:T(8,128)(2,1)}, u32[]{:S(2)}, u32[]{:S(2)}) async-start(bf16[16,8,4096]{2,1,0:T(8,128)(2,1)} %bitcast.48), calls=%async_computation | async-start | bytes 2097152 | tf_op jit(solution)/shard_map/all_to_all | solution.py:103
  12.6 0.1 reshape.103
  12.7 22.9 %all-to-all-done = bf16[16,8,4096]{2,1,0:T(8,128)(2,1)} async-done(((bf16[16,8,4096]{2,1,0:T(8,128)(2,1)}), bf16[16,8,4096]{2,1,0:T(8,128)(2,1)}, u32[]{:S(2)}, u32[]{:S(2)}) %all-to-all-start) | async-done | bytes 1048608 | tf_op jit(solution)/shard_map/all_to_all | solution.py:103
  35.6 0.0 copy-start.5
  35.6 3.1 %fusion.5 = f32[128,384]{1,0:T(8,128)S(1)} fusion(bf16[1,4096,384]{2,1,0:T(8,128)(2,1)} %param.15, bf16[16,8,4096]{2,1,0:T(8,128)(2,1)} %all-to-all-done), kind=kOutput, calls=%fused_computation.7 | convolution fusion | flops 402653184 | bytes 4390912 | tf_op jit(solution)/shard_map/dot_general | solution.py:61
  38.6 0.1 copy-done.5
  38.7 1.9 %fusion.11 = bf16[128,384]{1,0:T(8,128)(2,1)S(1)} fusion(bf16[1,4096,384]{2,1,0:T(8,128)(2,1)S(1)} %copy-done.5, bf16[16,8,4096]{2,1,0:T(8,128)(2,1)} %all-to-all-done, f32[128,384]{1,0:T(8,128)S(1)} %fusion.5), kind=kOutput, calls=%fused_computation.12 | convolution fusion | flops 402948096 | bytes 4489216 | tf_op jit(solution)/shard_map/dot_general | solution.py:62
  40.7 0.0 copy-done
  40.7 0.0 copy-start.7
  40.7 0.0 copy-start.2
  40.7 0.0 copy-start.6
  40.7 0.0 copy-start.1
  40.8 0.7 fusion.1
  41.5 0.1 select_bitcast_fusion
  41.6 0.7 collective-permute-start
  42.3 0.0 copy-done.7
  42.3 0.1 iota_compare_fusion.2
  42.3 0.0 copy-done.2
  42.3 0.0 copy-done.6
  42.3 0.1 fusion.26
  42.5 0.0 copy-done.1
  42.5 0.5 fusion.31
  43.0 0.0 copy-start.4
  43.0 0.0 copy-start.3
  43.0 0.2 fusion.19
  43.2 1.3 %collective-permute-done = f32[16,4,4096]{2,0,1:T(8,128)S(1)} collective-permute-done((f32[16,4,4096]{2,0,1:T(8,128)S(1)}, f32[16,4,4096]{2,0,1:T(8,128)S(1)}, u32[]{:S(2)}, u32[]{:S(2)}) %collective-permute-start) | collective-permute-done | bytes 1048608 | tf_op jit(solution)/shard_map/ppermute | solution.py:14
  44.5 0.1 fusion.16
  44.7 1.2 %copy.20 = bf16[16,4,4096]{2,1,0:T(4,128)(2,1)} copy(bf16[16,4,4096]{2,0,1:T(8,128)(2,1)S(1)} %fusion.16) | data formatting | bytes 1048576 | tf_op jit(solution)/shard_map/convert_element_type | solution.py:117
  45.9 6.7 %all-to-all-start.1 = ((bf16[16,4,4096]{2,1,0:T(4,128)(2,1)}), bf16[16,4,4096]{2,1,0:T(4,128)(2,1)}, u32[]{:S(2)}, u32[]{:S(2)}) async-start(bf16[16,4,4096]{2,1,0:T(4,128)(2,1)} %copy.20), calls=%async_computation.1 | async-start | bytes 1048576 | tf_op jit(solution)/shard_map/all_to_all | solution.py:118
  52.6 0.0 copy-done.4
  52.7 0.0 copy-done.3
  52.7 0.1 reduce_sum.36
  52.8 0.1 broadcast_divide_fusion
  52.9 2.2 %fusion.15 = bf16[4,4,16,128]{3,2,1,0:T(8,128)(2,1)} fusion(bf16[4,4,256,128]{3,2,1,0:T(8,128)(2,1)} %param.22, f32[4,4,16,256]{3,2,1,0:T(8,128)S(1)} %get-tuple-element.7, f32[4,4,16]{2,1,0:T(4,128)S(1)} %multiply_maximum_fusion, f32[4,4,16]{2,1,0:T(4,128)S(1)} %get-tuple-element.5, f32[4,4,128]{2,1,0:T(4,128)S(1)} %convert_element_type.43, ...), kind=kOutput, calls=%fused_computation.15 | convolution fusion | flops 17039360 | bytes 1387520 | tf_op jit(solution)/shard_map/skgc,skcd->skgd/dot_general | solution.py:38
  55.1 12.1 %all-to-all-done.1 = bf16[16,4,4096]{2,1,0:T(4,128)(2,1)} async-done(((bf16[16,4,4096]{2,1,0:T(4,128)(2,1)}), bf16[16,4,4096]{2,1,0:T(4,128)(2,1)}, u32[]{:S(2)}, u32[]{:S(2)}) %all-to-all-start.1) | async-done | bytes 524320 | tf_op jit(solution)/shard_map/all_to_all | solution.py:118
  67.1 2.0 %reshape.102 = bf16[64,4096]{1,0:T(8,128)(2,1)} reshape(bf16[16,4,4096]{2,1,0:T(4,128)(2,1)} %all-to-all-done.1) | data formatting | bytes 1048576 | tf_op jit(solution)/shard_map/reshape | solution.py:119
  69.1 3.3 %gather_fusion = bf16[64,4096]{1,0:T(8,128)(2,1)} fusion(bf16[64,4096]{1,0:T(8,128)(2,1)} %reshape.102, s32[1024]{0:T(1024)S(1)} %pad_clamp_fusion), kind=kCustom, calls=%fused_computation | custom fusion | bytes 1048832 | tf_op jit(solution)/shard_map/jit(_take)/gather | solution.py:121
  72.4 2.1 %multiply_reduce_fusion = bf16[8,4096]{1,0:T(8,128)(2,1)} fusion(bf16[64,4096]{1,0:T(8,128)(2,1)} %gather_fusion, f32[8,8]{1,0:T(8,128)S(1)} %broadcast_divide_fusion, pred[8,8]{1,0:T(8,128)(4,1)S(1)} %get-tuple-element.2), kind=kLoop, calls=%fused_computation.20 | loop fusion | flops 1015808 | bytes 590144 | tf_op jit(solution)/shard_map/reduce_sum | solution.py:126
  (7 shorter events, 0.1 us)
Async XLA Ops:
  0.6 40.1 %copy-start = (bf16[1,384,4096]{2,1,0:T(8,128)(2,1)S(1)}, bf16[1,384,4096]{2,1,0:T(8,128)(2,1)}, u32[]{:S(2)}) copy-start(bf16[1,384,4096]{2,1,0:T(8,128)(2,1)} %param.17) | copy-start | bytes 9437188
  5.1 30.4 %all-to-all-start = ((bf16[16,8,4096]{2,1,0:T(8,128)(2,1)}), bf16[16,8,4096]{2,1,0:T(8,128)(2,1)}, u32[]{:S(2)}, u32[]{:S(2)}) async-start(bf16[16,8,4096]{2,1,0:T(8,128)(2,1)} %bitcast.48), calls=%async_computation | async-start | bytes 2097152 | tf_op jit(solution)/shard_map/all_to_all | solution.py:103
  35.6 3.2 %copy-start.5 = (bf16[1,4096,384]{2,1,0:T(8,128)(2,1)S(1)}, bf16[1,4096,384]{2,1,0:T(8,128)(2,1)}, u32[]{:S(2)}) copy-start(bf16[1,4096,384]{2,1,0:T(8,128)(2,1)} %param.16) | copy-start | bytes 9437188
  40.7 1.6 %copy-start.7 = (s32[4]{0:T(128)S(1)}, s32[4]{0:T(128)}, u32[]{:S(2)}) copy-start(s32[4]{0:T(128)} %param.23) | copy-start | bytes 52
  40.7 1.6 %copy-start.2 = (bf16[4,64,128]{2,1,0:T(8,128)(2,1)S(1)}, bf16[4,64,128]{2,1,0:T(8,128)(2,1)}, u32[]{:S(2)}) copy-start(bf16[4,64,128]{2,1,0:T(8,128)(2,1)} %param.18) | copy-start | bytes 196612
  40.7 1.6 %copy-start.6 = (bf16[4,4,128]{2,1,0:T(4,128)(2,1)S(1)}, bf16[4,4,128]{2,1,0:T(4,128)(2,1)}, u32[]{:S(2)}) copy-start(bf16[4,4,128]{2,1,0:T(4,128)(2,1)} %param.19) | copy-start | bytes 12292
  40.7 1.7 %copy-start.1 = (bf16[4,4,256,128]{3,2,1,0:T(8,128)(2,1)S(1)}, bf16[4,4,256,128]{3,2,1,0:T(8,128)(2,1)}, u32[]{:S(2)}) copy-start(bf16[4,4,256,128]{3,2,1,0:T(8,128)(2,1)} %param.21) | copy-start | bytes 3145732
  41.6 3.0 %collective-permute-start = (f32[16,4,4096]{2,0,1:T(8,128)S(1)}, f32[16,4,4096]{2,0,1:T(8,128)S(1)}, u32[]{:S(2)}, u32[]{:S(2)}) collective-permute-start(f32[16,4,4096]{2,0,1:T(8,128)S(1)} %select_bitcast_fusion), channel_id=1, source_target_pairs={{0,1},{1,0},{2,3},{3,2},{4,5},{5,4},{6,7},{7,6},{8,9},{9,8},{10,11... | collective-permute-start | bytes 3145736 | tf_op jit(solution)/shard_map/ppermute | solution.py:14
  43.0 9.7 %copy-start.4 = (bf16[4,4,128]{2,1,0:T(4,128)(2,1)S(1)}, bf16[4,4,128]{2,1,0:T(4,128)(2,1)}, u32[]{:S(2)}) copy-start(bf16[4,4,128]{2,1,0:T(4,128)(2,1)} %param.20) | copy-start | bytes 12292
  43.0 9.7 %copy-start.3 = (f32[8,8]{1,0:T(8,128)S(1)}, f32[8,8]{1,0:T(8,128)}, u32[]{:S(2)}) copy-start(f32[8,8]{1,0:T(8,128)} %param.14) | copy-start | bytes 772
  45.9 21.2 %all-to-all-start.1 = ((bf16[16,4,4096]{2,1,0:T(4,128)(2,1)}), bf16[16,4,4096]{2,1,0:T(4,128)(2,1)}, u32[]{:S(2)}, u32[]{:S(2)}) async-start(bf16[16,4,4096]{2,1,0:T(4,128)(2,1)} %copy.20), calls=%async_computation.1 | async-start | bytes 1048576 | tf_op jit(solution)/shard_map/all_to_all | solution.py:118
where the time goes:
time: 75 us; the launch traced here: 74.5 us
  waiting for transfers between devices  36.3 us (48%)
  starting transfers between devices  14.8 us (20%)
  matrix products  9.69 us (13%)
  local copies, waits for them, and re-layouts  8.83 us (12%)
  other arithmetic  4.04 us (5%)
  between operations  0.83 us (1%)
    all_to_all x1, waiting for transfers between devices, body(): lax.all_to_all(doubled.reshape(node_count, capacity, model_width), 'node'...  22.9 us
    all_to_all x1, waiting for transfers between devices, body(): lax.all_to_all(summed, 'node', split_axis=0, concat_axis=0, tiled=True)  12.1 us
    all_to_all x1, starting transfers between devices, body(): lax.all_to_all(doubled.reshape(node_count, capacity, model_width), 'node'...  7.43 us
    all_to_all x1, starting transfers between devices, body(): lax.all_to_all(summed, 'node', split_axis=0, concat_axis=0, tiled=True)  6.68 us
    gather x1, local copies, waits for them, and re-layouts, body(): jnp.take(results, slot_codes.reshape(-1), axis=0)  3.27 us
    dot_general x1, matrix products, expert_layer(): jnp.dot(row_block, gate_weight[0], preferred_element_type=jnp.float32)  3.06 us
    dot_general x1, matrix products, attention_block(): jnp.einsum('skgc,skcd->skgd', prob_rows.astype(jnp.bfloat16), cache_value...  2.18 us
    reduce_sum x1, other arithmetic, body(): jnp.sum(share_norm[:, :, None] * picked, axis=1).astype(jnp.bfloat16)  2.11 us
  transfers between devices with their start and end apart: 3, of which 3 were waited for; matrix products, arithmetic and copies ran while one was open for 5% of the time, Pallas kernels for 0%

commit v1 on v0

v1 whole, which is shorter than its diff:
```python
import functools

import jax
import jax.numpy as jnp
from jax import lax
from jax.experimental import pallas as pl
from jax.experimental.pallas import tpu as pltpu
from jax.sharding import PartitionSpec as P

MESH = pl.DeviceIdType.MESH
F32 = jnp.float32
BF16 = jnp.bfloat16
PARTS = 4
LANES = 128
GROUP_BLOCKS = 16


def grid_of(node_count):
    chips = node_count // 2
    wide = 1
    while (2 * wide) * (2 * wide) <= chips and chips % (2 * wide) == 0:
        wide *= 2
    return chips // wide, wide


def kernel(
    tall, wide,
    x_ref, chosen_ref, route_ref, q_ref, fk_ref, fv_ref, len_ref,
    wg_hbm, wu_hbm, wd_hbm, ck_hbm, cv_hbm,
    mix_ref, att_ref,
    wg, wu, wd, ck, cv, gath, xs, hid, share,
    kept1, send1, recv1, kept2, send2, recv2, kept3, send3, recv3,
    load_sem, zs_sem, zr_sem, ys_sem, yr_sem, cs_sem, cr_sem,
    s1s, s1r, s2s, s2r, s3s, s3r,
):
    chips = tall * wide
    blocks = 2 * chips
    tokens, width = x_ref.shape
    half = width // 2
    part = half // PARTS
    me = lax.axis_index("node")
    core = me % 2
    y = (me // 2) % wide
    z = me // (2 * wide)

    def at_z(step):
        return {"node": ((z + step) % tall * wide + y) * 2 + core}

    def at_y(step):
        return {"node": (z * wide + (y + step) % wide) * 2 + core}

    partner = {"node": (z * wide + y) * 2 + 1 - core}

    loads = [
        pltpu.make_async_copy(src, dst, load_sem.at[i])
        for i, (src, dst) in enumerate(
            [(ck_hbm, ck), (cv_hbm, cv), (wg_hbm, wg), (wu_hbm, wu), (wd_hbm, wd)]
        )
    ]
    barrier = pltpu.get_barrier_semaphore()
    peers = [at_z(k) for k in range(1, tall)] + [at_y(j) for j in range(1, wide)] + [partner]
    for peer in peers:
        pl.semaphore_signal(barrier, inc=1, device_id=peer, device_id_type=MESH)
    for load in loads:
        load.start()

    route = route_ref[...]
    norm = route / jnp.sum(route, axis=1, keepdims=True)
    lane = lax.broadcasted_iota(jnp.int32, (tokens, LANES), 1)
    table = jnp.zeros((tokens, LANES), F32)
    chosen = chosen_ref[...]
    for k in range(chosen.shape[1]):
        table += jnp.where(lane == chosen[:, k : k + 1], norm[:, k : k + 1], 0.0)
    table_high = table.astype(BF16).astype(F32)
    xf = x_ref[...].astype(F32)
    gath[0, :, :half] = jnp.concatenate([xf[:, :half], xf[:, half:]], axis=0).astype(BF16)
    gath[0, :, half:] = jnp.concatenate([table_high, table - table_high], axis=0).astype(BF16)

    pl.semaphore_wait(barrier, len(peers))

    def block(dc, dy, dz):
        return (dc * wide + dy) * tall + dz

    sends = []

    def push(src, dst, ssem, rsem, device):
        copy = pltpu.make_async_remote_copy(
            src_ref=src, dst_ref=dst, send_sem=ssem, recv_sem=rsem,
            device_id=device, device_id_type=MESH,
        )
        copy.start()
        sends.append(copy)
        return copy

    z_copies = {}
    y_copies = {}
    c_copies = {}

    def to_y(dz):
        for j in range(1, wide):
            dy = wide - j
            i = dz * (wide - 1) + dy - 1
            y_copies[dy, dz] = push(
                gath.at[block(0, 0, dz)], gath.at[block(0, dy, dz)],
                ys_sem.at[i], yr_sem.at[i], at_y(j),
            )

    def to_core(dy, dz):
        i = dy * tall + dz
        c_copies[dy, dz] = push(
            gath.at[block(0, dy, dz)], gath.at[block(1, dy, dz)],
            cs_sem.at[i], cr_sem.at[i], partner,
        )

    to_y(0)
    for step in range(1, tall):
        k = (step + 1) // 2 if step % 2 else tall - step // 2
        dz = tall - k
        z_copies[dz] = push(
            gath.at[0], gath.at[dz], zs_sem.at[dz - 1], zr_sem.at[dz - 1], at_z(k)
        )
    to_core(0, 0)

    heads, head_width = ck.shape[1], ck.shape[3]
    context = ck.shape[2]
    seqs = ck.shape[0]
    group = q_ref.shape[1] // heads
    scaling = head_width ** (-0.5)

    def attend(s):
        queries = q_ref[s].reshape(heads, group, head_width)
        scores = (
            jnp.einsum("kgd,kcd->kgc", queries, ck[s], preferred_element_type=F32) * scaling
        )
        fk = fk_ref[s].astype(F32)
        own = (
            jnp.sum(queries.astype(F32) * fk[:, None, :], axis=2, keepdims=True) * scaling
        )
        column = lax.broadcasted_iota(jnp.int32, scores.shape, 2)
        masked = jnp.where(column < len_ref[s], scores, -jnp.inf)
        top = jnp.maximum(jnp.max(masked, axis=2, keepdims=True), own)
        prob = jnp.exp(masked - top)
        own_prob = jnp.exp(own - top)
        total = jnp.sum(prob, axis=2, keepdims=True) + own_prob
        mixed = jnp.einsum(
            "kgc,kcd->kgd", prob.astype(BF16), cv[s], preferred_element_type=F32
        )
        own_low = own_prob.astype(BF16).astype(F32)
        mixed = mixed + own_low * fv_ref[s].astype(F32)[:, None, :]
        att_ref[s] = (mixed / total).astype(BF16).reshape(heads * group, head_width)

    loads[0].wait()
    loads[1].wait()
    early = seqs // 2
    for s in range(early):
        attend(s)

    arrivals = []
    for step in range(1, tall):
        k = (step + 1) // 2 if step % 2 else tall - step // 2
        arrivals.append(tall - k)
    for dz in arrivals:
        z_copies[dz].wait_recv()
        to_y(dz)
        to_core(0, dz)
    for dz in [0] + arrivals:
        for dy in range(1, wide):
            y_copies[dy, dz].wait_recv()
            to_core(dy, dz)
    loads[2].wait()
    loads[3].wait()
    for dz in [0] + arrivals:
        for dy in range(wide):
            c_copies[dy, dz].wait_recv()

    per = min(blocks, GROUP_BLOCKS)
    rows = per * tokens
    expert = me // 2

    def first_half(start, at):
        for pair in range(per // 2):
            both = gath[pl.ds(start + 2 * pair, 2), :, :half].astype(F32)
            spot = pl.ds(pair * 2 * tokens, 2 * tokens)
            xs[spot, :half] = both[:, :tokens].reshape(2 * tokens, half).astype(BF16)
            xs[spot, half:] = both[:, tokens:].reshape(2 * tokens, half).astype(BF16)
        shares = gath[pl.ds(start, per), :, half:].astype(F32)
        shares = (shares[:, :tokens] + shares[:, tokens:]).reshape(rows, LANES)
        lanes = lax.broadcasted_iota(jnp.int32, (rows, LANES), 1)
        mine = jnp.sum(jnp.where(lanes == expert, shares, 0.0), axis=1, keepdims=True)
        share[pl.ds(at, rows), :] = jnp.broadcast_to(mine, (rows, LANES))
        gate = jnp.dot(xs[...], wg[0], preferred_element_type=F32)
        up = jnp.dot(xs[...], wu[0], preferred_element_type=F32)
        hid[pl.ds(at, rows), :] = (gate / (1.0 + jnp.exp(-gate)) * up).astype(BF16)

    groups = blocks // per
    if groups == 1:
        first_half(0, 0)
    else:

        @pl.loop(0, groups)
        def _(g):
            first_half(g * per, g * rows)

    loads[4].wait()

    def down(c, start, at):
        hidden = hid[pl.ds(at, rows), :]
        scale = share[pl.ds(at, rows), :1]
        sides = []
        for side in range(2):
            cols = pl.ds(side * half + c * part, part)
            out = jnp.dot(hidden, wd[0, :, cols], preferred_element_type=F32) * scale
            sides.append(out.reshape(per, tokens, part))
        return jnp.concatenate(sides, axis=1)

    def stage1(c):
        if groups == 1:
            out = down(c, 0, 0)
            send1[c] = out[chips:].astype(BF16)
            kept1[c] = out[:chips]
        else:

            @pl.loop(0, groups // 2)
            def _(g):
                send1[c, pl.ds(g * per, per)] = down(
                    c, chips + g * per, (groups // 2 + g) * rows
                ).astype(BF16)
                kept1[c, pl.ds(g * per, per)] = down(c, g * per, g * rows)

        return push(send1.at[c], recv1.at[c], s1s.at[c], s1r.at[c], partner)

    def stage2(c, before):
        before.wait_recv()
        copies = []
        for j in range(1, wide):
            span = pl.ds(j * tall, tall)
            send2[c, j - 1] = (kept1[c, span] + recv1[c, span].astype(F32)).astype(BF16)
            i = c * (wide - 1) + j - 1
            copies.append(
                push(send2.at[c, j - 1], recv2.at[c, j - 1], s2s.at[i], s2r.at[i], at_y(j))
            )
        span = pl.ds(0, tall)
        kept2[c] = kept1[c, span] + recv1[c, span].astype(F32)
        return copies

    def stage3(c, before):
        total = kept2[c]
        for j, copy in enumerate(before):
            copy.wait_recv()
            total = total + recv2[c, j].astype(F32)
        send3[c] = total[1:].astype(BF16)
        kept3[c] = total[0]
        copies = []
        for k in range(1, tall):
            i = c * (tall - 1) + k - 1
            copies.append(
                push(send3.at[c, k - 1], recv3.at[c, k - 1], s3s.at[i], s3r.at[i], at_z(k))
            )
        return copies

    def finish(c, before):
        total = kept3[c]
        for k, copy in enumerate(before):
            copy.wait_recv()
            total = total + recv3[c, k].astype(F32)
        mix_ref[:, pl.ds(c * part, part)] = total[:tokens].astype(BF16)
        mix_ref[:, pl.ds(half + c * part, part)] = total[tokens:].astype(BF16)

    ones, twos, threes = {}, {}, {}
    for c in range(PARTS):
        ones[c] = stage1(c)
        if c >= 1:
            twos[c - 1] = stage2(c - 1, ones[c - 1])
    twos[PARTS - 1] = stage2(PARTS - 1, ones[PARTS - 1])
    late = list(range(early, seqs))
    for c in range(PARTS):
        if late:
            attend(late.pop(0))
        threes[c] = stage3(c, twos[c])
    for s in late:
        attend(s)
    for c in range(PARTS):
        finish(c, threes[c])
    for copy in sends:
        copy.wait_send()


def body(
    mixer_input, chosen_experts, route_weight, gate_weight, up_weight, down_weight,
    queries, fresh_key, fresh_value, cache_key, cache_value, lengths,
):
    nodes = lax.axis_size("node")
    tall, wide = grid_of(nodes)
    chips = tall * wide
    tokens, width = mixer_input.shape
    hidden = gate_weight.shape[2]
    half = width // 2
    part = half // PARTS
    pair = 2 * tokens
    per = min(nodes, GROUP_BLOCKS)
    dma = pltpu.SemaphoreType.DMA
    vmem = pl.BlockSpec(memory_space=pltpu.VMEM)
    hbm = pl.BlockSpec(memory_space=pl.ANY)
    ys = max(1, wide - 1)
    zs = max(1, tall - 1)
    return pl.pallas_call(
        functools.partial(kernel, tall, wide),
        out_shape=(
            jax.ShapeDtypeStruct(mixer_input.shape, BF16),
            jax.ShapeDtypeStruct(queries.shape, BF16),
        ),
        in_specs=[vmem] * 6 + [pl.BlockSpec(memory_space=pltpu.SMEM)] + [hbm] * 5,
        out_specs=(vmem, vmem),
        scratch_shapes=[
            pltpu.VMEM(gate_weight.shape, BF16),
            pltpu.VMEM(up_weight.shape, BF16),
            pltpu.VMEM(down_weight.shape, BF16),
            pltpu.VMEM(cache_key.shape, BF16),
            pltpu.VMEM(cache_value.shape, BF16),
            pltpu.VMEM((nodes, pair, half + LANES), BF16),
            pltpu.VMEM((per * tokens, width), BF16),
            pltpu.VMEM((nodes * tokens, hidden), BF16),
            pltpu.VMEM((nodes * tokens, LANES), F32),
            pltpu.VMEM((PARTS, chips, pair, part), F32),
            pltpu.VMEM((PARTS, chips, pair, part), BF16),
            pltpu.VMEM((PARTS, chips, pair, part), BF16),
            pltpu.VMEM((PARTS, tall, pair, part), F32),
            pltpu.VMEM((PARTS, ys, tall, pair, part), BF16),
            pltpu.VMEM((PARTS, ys, tall, pair, part), BF16),
            pltpu.VMEM((PARTS, pair, part), F32),
            pltpu.VMEM((PARTS, zs, pair, part), BF16),
            pltpu.VMEM((PARTS, zs, pair, part), BF16),
            dma((5,)),
            dma((zs,)), dma((zs,)),
            dma((tall * ys,)), dma((tall * ys,)),
            dma((chips,)), dma((chips,)),
            dma((PARTS,)), dma((PARTS,)),
            dma((PARTS * ys,)), dma((PARTS * ys,)),
            dma((PARTS * zs,)), dma((PARTS * zs,)),
        ],
        compiler_params=pltpu.CompilerParams(
            collective_id=0, has_side_effects=True, vmem_limit_bytes=60 * 1024 * 1024
        ),
        name="moe_and_attention",
    )(
        mixer_input, chosen_experts, route_weight, queries, fresh_key, fresh_value, lengths,
        gate_weight, up_weight, down_weight, cache_key, cache_value,
    )


def solution(mesh):
    rows = P(("groups", "node"), None)
    node = P("node", None, None)
    seq3 = P(("groups", "node"), None, None)
    seq4 = P(("groups", "node"), None, None, None)
    in_specs = (
        rows, rows, rows, node, node, node,
        seq3, seq3, seq3, seq4, seq4, P(("groups", "node")),
    )
    return jax.shard_map(
        body, mesh=mesh, in_specs=in_specs, out_specs=(rows, seq3), check_vma=False
    )
```

time: 75 us -> 36.2 us (0.48)
  waiting for transfers between devices: 36.3 us -> 0 us
  Pallas kernels: 0 us -> 32.4 us
  starting transfers between devices: 14.8 us -> 0 us
  matrix products: 9.69 us -> 0 us
  local copies, waits for them, and re-layouts: 8.83 us -> 2.95 us
  other arithmetic: 4.04 us -> 0 us
    all_to_all x2 -> x0, waiting for transfers between devices: 35 us -> none  [the longest x1 22.9 us: body(): lax.all_to_all(doubled.reshape(node_count, capacity, model_width), 'node'...]
    pallas_call x0 -> x1, Pallas kernels: none -> 32.4 us  [body(): pl.pallas_call(functools.partial(kernel, tall, wide), out_shape=(jax.Shap...]
    all_to_all x2 -> x0, starting transfers between devices: 14.1 us -> none  [the longest x1 7.43 us: body(): lax.all_to_all(doubled.reshape(node_count, capacity, model_width), 'node'...]
    dot_general x7 -> x0, matrix products: 9.69 us -> none  [the longest x1 3.06 us: expert_layer(): jnp.dot(row_block, gate_weight[0], preferred_element_type=jnp.float32)]
    gather x1 -> x0, local copies, waits for them, and re-layouts: 3.27 us -> none  [body(): jnp.take(results, slot_codes.reshape(-1), axis=0)]
    unnamed x16 -> x2, local copies, waits for them, and re-layouts: 0.13 us -> 2.95 us
    reduce_sum x4 -> x0, other arithmetic: 2.62 us -> none  [the longest x1 2.11 us: body(): jnp.sum(share_norm[:, :, None] * picked, axis=1).astype(jnp.bfloat16)]
    reshape x3 -> x0, local copies, waits for them, and re-layouts: 2.13 us -> none  [the longest x1 1.97 us: body(): results = returned.reshape(expert_count * capacity, model_width)]
  transfers between devices with their start and end apart: 3 -> 0, of which waited for: 3 -> 0; matrix products, arithmetic and copies ran while one was open for 5% -> 0% of each run, Pallas kernels for 0% -> 0%
where the time goes in v1:
time: 36.2 us; the launch traced here: 36 us
  Pallas kernels  32.4 us (90%)
  local copies, waits for them, and re-layouts  2.95 us (8%)
  between operations  0.64 us (2%)
    pallas_call x1, Pallas kernels, body(): pl.pallas_call(functools.partial(kernel, tall, wide), out_shape=(jax.Shap...  32.4 us
    unnamed x2, local copies, waits for them, and re-layouts  2.95 us

profile of v1, /device:TPU:0, one launch (start us, length us, event | category | flops | bytes accessed | tf_op | source)
XLA Modules:
  0.0 36.0 jit_solution(4345090581683810939)
XLA Ops:
  0.6 32.4 %moe_and_attention.1 = (bf16[8,4096]{1,0:T(8,128)(2,1)}, bf16[4,64,128]{2,1,0:T(8,128)(2,1)}) custom-call(bf16[8,4096]{1,0:T(8,128)(2,1)} %x_ref.1, s32[8,8]{1,0:T(8,128)} %chosen_ref.1, f32[8,8]{1,0:T(8,128)} %route_ref.1, bf16[4,64,128]{2,1,0:T(8,128)(2,1)} %q_ref.1, bf16[4,4,128]{2,1,0:T(4,128)(2,1)} %fk_ref.1, bf16[4,4,128]{2,1,0:T(4,128)(2,1)} %fv_ref.1, ...), custom_call_target="tpu_custom_call" | custom-call | tf_op jit(solution)/shard_map/moe_and_attention/pallas_call | solution.py:306
  33.0 1.5 %copy.16 = bf16[8,4096]{1,0:T(8,128)(2,1)} copy(bf16[8,4096]{1,0:T(8,128)(2,1)} %get-tuple-element.4) | data formatting | bytes 131072
  34.5 1.5 %copy.17 = bf16[4,64,128]{2,1,0:T(8,128)(2,1)} copy(bf16[4,64,128]{2,1,0:T(8,128)(2,1)} %get-tuple-element.5) | data formatting | bytes 131072

commit v2 on v1

--- a/solution.py
+++ b/solution.py
@@ -285,6 +285,11 @@
         copy.wait_send()
 
 
+def place(mix_in, att_in, mix_out, att_out):
+    mix_out[...] = mix_in[...]
+    att_out[...] = att_in[...]
+
+
 def body(
     mixer_input, chosen_experts, route_weight, gate_weight, up_weight, down_weight,
     queries, fresh_key, fresh_value, cache_key, cache_value, lengths,
@@ -303,7 +308,7 @@
     hbm = pl.BlockSpec(memory_space=pl.ANY)
     ys = max(1, wide - 1)
     zs = max(1, tall - 1)
-    return pl.pallas_call(
+    mixture, attended = pl.pallas_call(
         functools.partial(kernel, tall, wide),
         out_shape=(
             jax.ShapeDtypeStruct(mixer_input.shape, BF16),
@@ -346,6 +351,16 @@
         mixer_input, chosen_experts, route_weight, queries, fresh_key, fresh_value, lengths,
         gate_weight, up_weight, down_weight, cache_key, cache_value,
     )
+    return pl.pallas_call(
+        place,
+        out_shape=(
+            jax.ShapeDtypeStruct(mixture.shape, BF16),
+            jax.ShapeDtypeStruct(attended.shape, BF16),
+        ),
+        in_specs=[vmem] * 2,
+        out_specs=(vmem, vmem),
+        name="place_results",
+    )(mixture, attended)
 
 
 def solution(mesh):

time: 36.2 us -> 34.7 us (0.959)
  local copies, waits for them, and re-layouts: 2.95 us -> 0 us
  Pallas kernels: 32.4 us -> 33.9 us
    unnamed x2 -> x0, local copies, waits for them, and re-layouts: 2.95 us -> none
    pallas_call x0 -> x1, Pallas kernels: none -> 1.53 us  [body(): pl.pallas_call(place, out_shape=(jax.ShapeDtypeStruct(mixture.shape, BF16...]
where the time goes in v2:
time: 34.7 us; the launch traced here: 34.5 us
  Pallas kernels  33.9 us (98%)
  between operations  0.64 us (2%)
    pallas_call x1, Pallas kernels, body(): pl.pallas_call(functools.partial(kernel, tall, wide), out_shape=(jax.Shap...  32.4 us
    pallas_call x1, Pallas kernels, body(): pl.pallas_call(place, out_shape=(jax.ShapeDtypeStruct(mixture.shape, BF16...  1.53 us

profile of v2, /device:TPU:0, one launch (start us, length us, event | category | flops | bytes accessed | tf_op | source)
XLA Modules:
  0.0 34.5 jit_solution(1931984779451977508)
XLA Ops:
  0.6 32.4 %moe_and_attention.1 = (bf16[8,4096]{1,0:T(8,128)(2,1)}, bf16[4,64,128]{2,1,0:T(8,128)(2,1)}) custom-call(bf16[8,4096]{1,0:T(8,128)(2,1)} %x_ref.1, s32[8,8]{1,0:T(8,128)} %chosen_ref.1, f32[8,8]{1,0:T(8,128)} %route_ref.1, bf16[4,64,128]{2,1,0:T(8,128)(2,1)} %q_ref.1, bf16[4,4,128]{2,1,0:T(4,128)(2,1)} %fk_ref.1, bf16[4,4,128]{2,1,0:T(4,128)(2,1)} %fv_ref.1, ...), custom_call_target="tpu_custom_call" | custom-call | tf_op jit(solution)/shard_map/moe_and_attention/pallas_call | solution.py:311
  33.0 1.5 %place_results.1 = (bf16[8,4096]{1,0:T(8,128)(2,1)}, bf16[4,64,128]{2,1,0:T(8,128)(2,1)}) custom-call(bf16[8,4096]{1,0:T(8,128)(2,1)} %get-tuple-element.4.mix_in, bf16[4,64,128]{2,1,0:T(8,128)(2,1)} %get-tuple-element.5.att_in), custom_call_target="tpu_custom_call" | custom-call | tf_op jit(solution)/shard_map/place_results/pallas_call | solution.py:354
